TPU v7x, 256 devices: a whole 4x4x8 slice. The times are simulated.
256 devices in a mesh: band: 8 (over x, y_lo), fft: 32 (over z, y_hi, core).
Axes of the slice: x: 4, y: 4 (y_hi: 2, y_lo: 2; y = y_hi * 2 + y_lo), z: 8, core: 2. Of those that a mesh axis runs over, the one named last changes fastest.
Arguments:
- orbitals: float32 [32, 5184, 216], P('band', 'fft'), may hold values from -6 to 6
- picked: int32 [8], P('band'), may hold values from 0 to 3, as said below
- shells: int32 [64], replicated, may hold values 0 or 1
Outputs:
- potentials: float32 [8, 5184, 216], P('band', 'fft')
- intersection: float32 [32, 1], P('band')
Inputs may be any that keep to these rules, and one draw needn't show every extreme that they name: `picked`: within each group's 1 entries the bands named are distinct; every value from 0 to 3 is named by some group.
All inputs are finite; a program needn't handle non-finite values.
Results may differ from a plain program's by a relative error of at most 0.0003.
Values sent between devices are 32-bit elements; how exact they have to be, the bound alone decides.
A program may use at most 128 MiB of HBM per device.

v0:
```python
import math

import jax
import jax.numpy as jnp
import numpy as np
from jax import lax
from jax.experimental import pallas as pl
from jax.experimental.pallas import tpu as pltpu
from jax.sharding import PartitionSpec as P

NX = 72
NY = 72
NZ = 216
BLK = 4
NSHELL = 64
FIELDS = 7
FFT = 32
ROWS = 162
MAIN = 128
TAIL = ROWS - MAIN
SLABS = 9
PLANES = 13

SPACING = 0.2
SCREENING = 0.106
FRACTION = 0.25
SPAN = math.lcm(NX, NY, NZ)
QTOP = (SPAN // NX) ** 2 * (NX // 2) ** 2 + (SPAN // NY) ** 2 * (NY // 2) ** 2 + (SPAN // NZ) ** 2 * (NZ // 2) ** 2
MESH = pl.DeviceIdType.MESH
F32 = jnp.float32
BF16 = jnp.bfloat16
VMEM_LIMIT = 60 * 1024 * 1024


def halves(table):
    table = np.asarray(table, np.float32)
    high = table.astype(jnp.bfloat16)
    low = (table - high.astype(np.float32)).astype(jnp.bfloat16)
    return high, low


def z_tables():
    freq, is_sin = np.zeros(NZ, np.int64), np.zeros(NZ, bool)
    for t in range(NZ // 8):
        for i in range(4):
            freq[8 * t + i] = 4 * t + i
            freq[8 * t + 4 + i] = 4 * t + i
            is_sin[8 * t + 4 + i] = True
    freq[4], is_sin[4] = NZ // 2, False
    angle = 2 * np.pi * (freq[:, None] * np.arange(NZ)[None, :] % NZ) / NZ
    forward = np.where(is_sin[:, None], -np.sin(angle), np.cos(angle))
    weight = np.where((freq == 0) | (freq == NZ // 2), 1.0, 2.0) / (NX * NY * NZ)
    inverse = (-FRACTION * weight[:, None] * forward).T
    return forward, inverse


def z_stacks():
    forward, inverse = z_tables()
    pad = np.zeros((8, NZ), jnp.bfloat16)

    def stack(table):
        high, low = halves(table)
        return np.concatenate([high, pad, low, pad], axis=0)

    return stack(forward), stack(inverse)


def xy_angle():
    index = np.arange(NX)
    return 2 * np.pi * (index[:, None] * index[None, :] % NX) / NX


def x_table():
    table = np.concatenate([np.cos(xy_angle()), np.sin(xy_angle())], axis=0)
    high, low = halves(table)
    pad = np.zeros((2 * NX, 8), high.dtype)
    return np.concatenate([high, pad, low, pad, high, pad], axis=1)


def y_tables():
    cosine, sine = np.cos(xy_angle()), np.sin(xy_angle())
    forward = np.zeros((256, 256))
    forward[:NY, :NY] = cosine
    forward[128:128 + NY, 128:128 + NY] = cosine
    forward[:NY, 128:128 + NY] = -sine
    forward[128:128 + NY, :NY] = sine
    fh, fl = halves(forward)
    return np.stack([fh, fl, fh.T, fl.T])


def xy_square():
    index = np.arange(NX)
    signed = np.where(index > NX // 2, index - NX, index)
    square = np.zeros((NX, 128), np.float32)
    square[:, :NY] = 9 * (signed[:, None] ** 2 + signed[None, :] ** 2)
    return square


def split(value):
    high = value.astype(BF16)
    return high, (value - high.astype(F32)).astype(BF16)


def mm(left, right):
    return lax.dot_general(left, right, (((1,), (0,)), ((), ())), preferred_element_type=F32)


def lanes(shape):
    return lax.broadcasted_iota(jnp.int32, shape, len(shape) - 1)


def turn(value, shift):
    shift = shift % 128
    return value if shift == 0 else pltpu.roll(value, shift, 1)


def pack_tail(parts):
    lane = lanes(parts[0].shape)
    upper = jnp.where(lane < 2 * TAIL, turn(parts[1], TAIL), turn(parts[2], 2 * TAIL))
    return jnp.where(lane < TAIL, parts[0], upper)


def pack_thirds(tail):
    third = NZ // 3
    return pack_tail([tail[third * g:third * (g + 1)] for g in range(3)])


def pack_field(wide):
    return jnp.concatenate([wide[:, :MAIN], pack_thirds(wide[:, MAIN:])], axis=0)


def unpack_field(packed):
    tail = packed[NZ:]
    tails = jnp.concatenate([turn(tail, -TAIL * g) for g in range(3)], axis=0)
    return jnp.concatenate([packed[:NZ], tails], axis=1)


def z_transform(table_ref, wide):
    high, low = split(wide)
    both = mm(table_ref[...], high)
    return both[:NZ] + both[NZ + 8:2 * NZ + 8] + mm(table_ref[:NZ + 8], low)[:NZ]


def order_bands(picked, orbitals_ref, own_ref, order_ref, pad_ref):
    pad_ref[...] = jnp.zeros_like(pad_ref)
    for b in range(BLK):
        pad_ref[:ROWS, :NZ] = orbitals_ref[:, b, :]
        own_ref[b] = pack_field(jnp.transpose(pad_ref[...])[:NZ])
    chosen = own_ref[0]
    for b in range(1, BLK):
        chosen = jnp.where(picked == b, own_ref[b], chosen)
    order_ref[0] = chosen


def order_others(picked, own_ref, order_ref):
    for j in range(1, BLK):
        order_ref[j] = jnp.where(picked >= j, own_ref[j - 1], own_ref[j])


def visitor_of(f):
    return (True, f + 1) if f < 3 else (False, f - 3)


def cuts_of(f):
    result = []
    for chunk in range(2):
        low, high = max(NZ * f, 768 * chunk), min(NZ * (f + 1), 768 * (chunk + 1))
        if low < high:
            result.append((low, high - low, low + 256 * chunk))
    return result


def runs(row, rows):
    tile, count = row // 8, rows // 8
    done = 0
    while done < count:
        place, peer = divmod(tile + done, FFT)
        take = min(count - done, FFT - peer)
        yield place // 4, place % 4, peer, take, done
        done += take


def put_rows(buffer, row, value):
    tiles = value.reshape(value.shape[0] // 8, 8, 128)
    for chunk, part, peer, take, done in runs(row, value.shape[0]):
        buffer[chunk, peer:peer + take, part] = tiles[done:done + take]


def get_rows(buffer, row, rows):
    parts = [buffer[chunk, peer:peer + take, part].reshape(8 * take, 128) for chunk, part, peer, take, _ in runs(row, rows)]
    return parts[0] if len(parts) == 1 else jnp.concatenate(parts, axis=0)


def spectrum_of(f, order_ref, upper_ref, lower_ref, table_ref, buffer, tail_ref):
    low_side, j = visitor_of(f)
    density = (lower_ref if low_side else upper_ref)[...] * order_ref[j]
    spectrum = z_transform(table_ref, unpack_field(density))
    for low, count, place in cuts_of(f):
        first = low - NZ * f
        put_rows(buffer, place, spectrum[first:first + count, :MAIN])
        tail_ref[pl.ds(low, count), :] = spectrum[first:first + count, MAIN:]


def close_tails(chunk, buffer, tail_ref):
    parts = [tail_ref[pl.ds(768 * chunk + 256 * p, 256), :] for p in range(3)]
    put_rows(buffer, 1024 * chunk + 768, pack_tail(parts))


def open_tails(chunk, buffer, tail_ref):
    tails = get_rows(buffer, 1024 * chunk + 768, 256)
    for p in range(3):
        tail_ref[pl.ds(768 * chunk + 256 * p, 256), :] = turn(tails, -TAIL * p)


def main_of(f, buffer):
    mains = [get_rows(buffer, place, count) for _, count, place in cuts_of(f)]
    return mains[0] if len(mains) == 1 else jnp.concatenate(mains, axis=0)


def tail_of(f, tail_ref):
    return tail_ref[pl.ds(NZ * f, NZ), :]


def pieces():
    result = []
    row = 0
    while row < 4 * ROWS:
        source, j = divmod(row, ROWS)
        slab, y = divmod(row, NY)
        stop = min((source + 1) * ROWS, (slab + 1) * NY)
        if j < MAIN:
            stop = min(stop, source * ROWS + MAIN)
        result.append((source, j >= MAIN, j if j < MAIN else j - MAIN, slab, y, stop - row))
        row = stop
    return result


def tile_of(owner, chunk, p):
    return lax.rem(96 * chunk + 32 * p + owner, NZ // 8)


def gain_of(owner, plane, shells_ref, xy_ref, gain):
    chunk, place = plane // PLANES, lax.rem(plane, PLANES)
    depth = jnp.where(place == PLANES - 1, NZ // 2, 4 * tile_of(owner, chunk, place // 4) + lax.rem(place, 4))
    square = xy_ref[...] + (depth * depth).astype(F32)
    total = jnp.full(square.shape, shells_ref[0].astype(F32), F32)
    for s in range(1, NSHELL):
        step = (shells_ref[s] - shells_ref[s - 1]).astype(F32)
        total = total + jnp.where(square >= float(-(-s * (QTOP + 1) // NSHELL)), step, 0.0)
    g_squared = (2.0 * math.pi / (SPACING * SPAN)) ** 2 * square
    safe = jnp.where(square == 0, 1.0, g_squared)
    value = 4.0 * math.pi / safe * (1.0 - jnp.exp(-safe / (4.0 * SCREENING**2)))
    gain[pl.ds(pl.multiple_of(plane * NX, 8), NX), :] = total * jnp.where(square == 0, math.pi / SCREENING**2, value)


def open_rows(got_ref, chunk, box):
    cuts = pieces()
    lane = lanes((8, 128))

    def one(chip, carry):
        for slab in range(SLABS):
            mine = [c for c in cuts if c[3] == slab]
            for p in range(3):
                value = None
                for source, tail, first, _, y, _ in mine:
                    part = got_ref[chunk, 4 * chip + source, 3 if tail else p]
                    part = turn(part, y - first - (TAIL * p if tail else 0))
                    value = part if value is None else jnp.where(lane >= y, part, value)
                box[pl.ds(8 * p * NX + SLABS * chip + slab, 8, stride=NX), :] = value
        return carry

    lax.fori_loop(0, 8, one, 0)


def close_rows(box, chunk, send_ref):
    cuts = pieces()
    lane = lanes((8, 128))

    def one(chip, carry):
        fields = [[box[pl.ds(8 * p * NX + SLABS * chip + slab, 8, stride=NX), :] for slab in range(SLABS)] for p in range(3)]
        for source in range(4):
            tail_value = None
            for p in range(3):
                value = None
                for s, tail, first, slab, y, _ in cuts:
                    if s != source:
                        continue
                    if tail:
                        place = first + TAIL * p
                        part = turn(fields[p][slab], place - y)
                        tail_value = part if tail_value is None else jnp.where(lane >= place, part, tail_value)
                    else:
                        part = turn(fields[p][slab], first - y)
                        value = part if value is None else jnp.where(lane >= first, part, value)
                send_ref[chunk, 4 * chip + source, p] = value
            send_ref[chunk, 4 * chip + source, 3] = tail_value
        return carry

    lax.fori_loop(0, 8, one, 0)


def screen_planes(owner, chunk, x_ref, y_ref, box, work, gain):
    flags = [jnp.where(tile_of(owner, chunk, p) == 0, 1.0, 0.0).astype(F32) for p in range(3)]

    def along_x(real, imag):
        wide = jnp.concatenate([real, imag], axis=1)
        wide = jnp.concatenate([wide, jnp.zeros((8, 256), F32)], axis=0)
        high, low = split(wide)
        both = mm(x_ref[...], jnp.concatenate([high, high, low], axis=0))
        return both[:NX, :128], both[:NX, 128:], both[NX:, :128], both[NX:, 128:]

    def along_y(value, k):
        high, low = split(value)
        return mm(high, y_ref[k]) + mm(low, y_ref[k]) + mm(high, y_ref[k + 1])

    for plane in range(PLANES):
        if plane == 12:
            real = sum(flags[p] * box[pl.ds((8 * p + 4) * NX, NX), :] for p in range(3))
            imag = jnp.zeros_like(real)
        else:
            p, i = divmod(plane, 4)
            real = box[pl.ds((8 * p + i) * NX, NX), :]
            imag = box[pl.ds((8 * p + 4 + i) * NX, NX), :]
            if i == 0:
                imag = imag * (1.0 - flags[p])
        cr, ci, sr, si = along_x(real, imag)
        work[pl.ds(plane * NX, NX), :] = jnp.concatenate([cr + si, ci - sr], axis=1)
    weight = gain[pl.ds(chunk * PLANES * NX, PLANES * NX), :]
    value = along_y(work[...], 0) * jnp.concatenate([weight, weight], axis=1)
    work[...] = along_y(value, 2)
    extra = None
    for plane in reversed(range(PLANES)):
        rows = work[pl.ds(plane * NX, NX), :]
        cr, ci, sr, si = along_x(rows[:, :128], rows[:, 128:])
        real, imag = cr - si, ci + sr
        if plane == 12:
            extra = real
        else:
            p, i = divmod(plane, 4)
            if i == 0:
                imag = imag * (1.0 - flags[p]) + extra * flags[p]
            box[pl.ds((8 * p + i) * NX, NX), :] = real
            box[pl.ds((8 * p + 4 + i) * NX, NX), :] = imag


def intersect(total, bands_ref, partial_ref):
    lines = []
    for b in range(BLK):
        product = (bands_ref[b] * total).reshape(36, 8, 128)
        line = jnp.sum(jnp.sum(product, axis=0), axis=0, keepdims=True)
        line = line + turn(line, 64)
        lines.append(line + turn(line, 32))
    quarter = lanes((1, 128)) // 32
    row = lines[0]
    for b in range(1, BLK):
        row = jnp.where(quarter == b, lines[b], row)
    partial_ref[...] = row * SPACING**3


STEPS = [(far, turned) for turned in range(4) for far in (4, 1, -1, 2, -2, 3, -3)] + [(0, turned) for turned in range(1, 4)]


class Ring:
    def __init__(self, me, source, target, send_sem, recv_sem):
        self.source, self.target = source, target
        self.send_sem, self.recv_sem = send_sem, recv_sem
        self.me = me
        self.places = [lax.rem(me // 4 + k, 8) for k in range(8)]
        self.parts = [lax.rem(lax.rem(me, 4) + k, 4) for k in range(4)]

    def device(self, far, turned):
        return 4 * self.places[far % 8] + self.parts[turned % 4]

    def copy(self, source, target, peer, k):
        return pltpu.make_async_remote_copy(
            src_ref=source, dst_ref=target, send_sem=self.send_sem.at[k], recv_sem=self.recv_sem.at[k],
            device_id={"fft": peer}, device_id_type=MESH,
        )

    def start(self, chunk, first, count, k):
        rows = pl.ds(first, count)
        for far, turned in STEPS:
            peer = self.device(far, turned)
            self.copy(self.source.at[chunk, peer, rows], self.target.at[chunk, self.me, rows], peer, k).start()
        self.target[chunk, self.me, first:first + count] = self.source[chunk, self.me, first:first + count]

    def wait_recv(self, chunk, first, count, k):
        whole = self.target.at[chunk, pl.ds(0, FFT - 1), pl.ds(first, count)]
        self.copy(whole, whole, self.device(1, 0), k).wait_recv()

    def wait_send(self, chunk, first, count, k):
        whole = self.source.at[chunk, pl.ds(0, FFT - 1), pl.ds(first, count)]
        self.copy(whole, whole, self.device(1, 0), k).wait_send()


def whole_kernel(
    picked_ref, shells_ref, orbitals_far, forward_far, inverse_far, xy_far, x_far, y_far,
    total_ref, result_ref,
    orbitals_ref, forward_ref, inverse_ref, xy_ref, x_ref, y_ref, fetch_sem,
    own, order, upper, lower, up, down, above, below, mine, sent, got, back, returned, tails, box, work, gain, pad,
    partial, ring_slots, near, near_slots,
    there_send, there_recv, home_send, home_recv, band_send, band_recv, ring_send, ring_recv, near_send, near_recv,
):
    me = lax.axis_index("fft")
    group = lax.axis_index("band")
    count = lax.axis_size("band")
    above_me, below_me = lax.rem(group + 1, count), lax.rem(group + count - 1, count)

    barrier = pltpu.get_barrier_semaphore()
    for peer in (above_me, below_me):
        pl.semaphore_signal(barrier, inc=1, device_id={"band": peer}, device_id_type=MESH)
    there = Ring(me, sent, got, there_send, there_recv)
    home = Ring(me, back, returned, home_send, home_recv)
    for far, turned in STEPS:
        peer = there.device(far, turned)
        pl.semaphore_signal(barrier, inc=1, device_id={"fft": peer}, device_id_type=MESH)

    def to_band(source, target, peer, k):
        return pltpu.make_async_remote_copy(
            src_ref=source, dst_ref=target, send_sem=band_send.at[k], recv_sem=band_recv.at[k],
            device_id={"band": peer}, device_id_type=MESH,
        )

    chosen_up = to_band(order.at[0], lower, above_me, 0)
    chosen_down = to_band(order.at[0], upper, below_me, 1)
    sum_down = to_band(down, above, below_me, 2)
    main, tail = pl.ds(0, NZ), pl.ds(NZ, NZ // 3)
    sum_up_main = to_band(up.at[main], below.at[main], above_me, 3)
    sum_up_tail = to_band(up.at[tail], below.at[tail], above_me, 4)

    fetches = [
        pltpu.make_async_copy(far, ref, fetch_sem.at[k])
        for k, (far, ref) in enumerate(
            [
                (orbitals_far, orbitals_ref), (xy_far, xy_ref), (forward_far, forward_ref),
                (x_far, x_ref), (y_far, y_ref), (inverse_far, inverse_ref),
            ]
        )
    ]
    for one in fetches:
        one.start()
    picked = picked_ref[0]
    fetches[0].wait()
    order_bands(picked, orbitals_ref, own, order, pad)
    pl.semaphore_wait(barrier, FFT + 1)
    chosen_up.start()
    order_others(picked, own, order)

    def gain_step(plane, carry):
        gain_of(me, plane, shells_ref, xy_ref, gain)
        return carry

    for one in fetches[1:]:
        one.wait()
    lax.fori_loop(0, 6, gain_step, 0)
    chosen_down.start()
    lax.fori_loop(6, 10, gain_step, 0)
    tails[pl.ds(NZ * FIELDS, 24), :] = jnp.zeros((24, 128), F32)
    put_rows(sent, NZ * FIELDS + 256, jnp.zeros((24, 128), F32))

    chosen_up.wait_recv()
    for f in range(3):
        spectrum_of(f, order, upper, lower, forward_ref, sent, tails)
    there.start(0, 0, 2, 0)
    chosen_down.wait_recv()
    spectrum_of(3, order, upper, lower, forward_ref, sent, tails)
    close_tails(0, sent, tails)
    there.start(0, 2, 2, 0)
    for f in range(4, FIELDS):
        spectrum_of(f, order, upper, lower, forward_ref, sent, tails)
    close_tails(1, sent, tails)
    there.start(1, 0, 4, 1)
    lax.fori_loop(10, 2 * PLANES, gain_step, 0)

    for chunk in range(2):
        there.wait_recv(chunk, 0, 4, chunk)
        open_rows(got, chunk, box)
        screen_planes(me, chunk, x_ref, y_ref, box, work, gain)
        close_rows(box, chunk, back)
        if chunk == 0:
            home.start(0, 0, 4, 0)
        else:
            home.start(1, 0, 3, 1)
            home.start(1, 3, 1, 2)

    home.wait_recv(0, 0, 4, 0)
    open_tails(0, returned, tails)
    total = None
    for f in range(3):
        field = pack_field(z_transform(inverse_ref, jnp.concatenate([main_of(f, returned), tail_of(f, tails)], axis=1)))
        term = field * order[visitor_of(f)[1]]
        total = term if total is None else total + term
    down[...] = total
    sum_down.start()

    def up_part(rows, fields):
        total = None
        for f, field in fields:
            if f == 3:
                mine[rows, :] = field * upper[rows, :]
            term = field * order[visitor_of(f)[1], rows, :]
            total = term if total is None else total + term
        up[rows, :] = total

    home.wait_recv(1, 0, 3, 1)
    up_part(main, [(f, z_transform(inverse_ref, main_of(f, returned))) for f in range(3, FIELDS)])
    sum_up_main.start()
    home.wait_recv(1, 3, 1, 2)
    open_tails(1, returned, tails)
    up_part(tail, [(f, pack_thirds(z_transform(inverse_ref, tail_of(f, tails)))) for f in range(3, FIELDS)])
    sum_up_tail.start()
    sum_down.wait_recv()
    mine[...] += above[...]
    sum_up_main.wait_recv()
    sum_up_tail.wait_recv()
    total = mine[...] + below[...]
    total_ref[...] = total
    intersect(total, own, partial)

    place, part = me // 4, lax.rem(me, 4)

    def row_to(source, target, peer, send_sem, recv_sem):
        return pltpu.make_async_remote_copy(
            src_ref=source, dst_ref=target, send_sem=send_sem, recv_sem=recv_sem,
            device_id={"fft": peer}, device_id_type=MESH,
        )

    ring = [
        row_to(partial, ring_slots.at[k], 4 * lax.rem(place + k, 8) + part, ring_send.at[k], ring_recv.at[k])
        for k in range(1, 8)
    ]
    for one in ring:
        one.start()
    row = partial[...]
    for k, one in enumerate(ring):
        one.wait()
        row = row + ring_slots[k + 1]
    near[...] = row
    beside = [
        row_to(near, near_slots.at[k], 4 * place + lax.rem(part + k, 4), near_send.at[k], near_recv.at[k])
        for k in range(1, 4)
    ]
    for one in beside:
        one.start()
    for k, one in enumerate(beside):
        one.wait()
        row = row + near_slots[k + 1]
    result_ref[...] = row

    there.wait_send(0, 0, 4, 0)
    there.wait_send(1, 0, 4, 1)
    home.wait_send(0, 0, 4, 0)
    home.wait_send(1, 0, 3, 1)
    home.wait_send(1, 3, 1, 2)
    for one in (chosen_up, chosen_down, sum_down, sum_up_main, sum_up_tail):
        one.wait_send()


def last_kernel(total_ref, row_ref, potential_ref, result_ref, pad_ref):
    pad_ref[...] = jnp.zeros_like(pad_ref)
    pad_ref[:NZ, :] = unpack_field(total_ref[...])
    potential_ref[:, 0, :] = jnp.transpose(pad_ref[...])[:ROWS, :NZ]
    row = row_ref[...]
    lane = lanes((1, BLK))
    result = jnp.zeros((1, BLK), F32)
    for b in range(BLK):
        mine = lanes((1, 128)) // 32 == b
        result = jnp.where(lane == b, jnp.sum(jnp.where(mine, row, 0.0), axis=1, keepdims=True), result)
    result_ref[...] = result


def vm():
    return pl.BlockSpec(memory_space=pltpu.VMEM)


def sm():
    return pl.BlockSpec(memory_space=pltpu.SMEM)


def params(**extra):
    return pltpu.CompilerParams(vmem_limit_bytes=VMEM_LIMIT, **extra)


def shape(*dims):
    return jax.ShapeDtypeStruct(dims, F32)


def body(orbitals, picked, shells):
    forward, inverse = z_stacks()
    along_x, along_y = x_table(), y_tables()
    exchange = pltpu.VMEM((2, FFT, 4, 8, 128), F32)
    field = pltpu.VMEM((288, 128), F32)
    bands = pltpu.VMEM((BLK, 288, 128), F32)
    line = pltpu.VMEM((1, 128), F32)
    dma = pltpu.SemaphoreType.DMA
    total, row = pl.pallas_call(
        whole_kernel,
        out_shape=(shape(288, 128), shape(1, 128)),
        in_specs=[sm(), sm()] + [pl.BlockSpec(memory_space=pl.ANY)] * 6,
        out_specs=(vm(), vm()),
        scratch_shapes=[
            pltpu.VMEM((ROWS, BLK, NZ), F32),
            pltpu.VMEM(forward.shape, BF16),
            pltpu.VMEM(inverse.shape, BF16),
            pltpu.VMEM((NX, 128), F32),
            pltpu.VMEM(along_x.shape, BF16),
            pltpu.VMEM(along_y.shape, BF16),
            dma((6,)),
            bands,
            bands,
        ]
        + [field] * 7
        + [exchange] * 4
        + [
            pltpu.VMEM((1536, 128), F32),
            pltpu.VMEM((24 * NX, 128), F32),
            pltpu.VMEM((PLANES * NX, 256), F32),
            pltpu.VMEM((2 * PLANES * NX, 128), F32),
            pltpu.VMEM((256, 256), F32),
            line,
            pltpu.VMEM((8, 1, 128), F32),
            line,
            pltpu.VMEM((4, 1, 128), F32),
        ]
        + [dma((2,))] * 2
        + [dma((3,))] * 2
        + [dma((5,))] * 2
        + [dma((8,))] * 2
        + [dma((4,))] * 2,
        compiler_params=params(collective_id=0, has_side_effects=True),
    )(
        picked, shells, jnp.transpose(orbitals, (1, 0, 2)), jnp.asarray(forward), jnp.asarray(inverse),
        jnp.asarray(xy_square()), jnp.asarray(along_x), jnp.asarray(along_y),
    )
    potentials, result = pl.pallas_call(
        last_kernel,
        out_shape=(shape(ROWS, 1, NZ), shape(1, BLK)),
        in_specs=[vm()] * 2,
        out_specs=(vm(), vm()),
        scratch_shapes=[pltpu.VMEM((256, 256), F32)],
        compiler_params=params(),
    )(total, row)
    return jnp.transpose(potentials, (1, 0, 2)), jnp.transpose(result)


def solution(mesh):
    return jax.shard_map(
        body,
        mesh=mesh,
        in_specs=(P("band", "fft", None), P("band"), P()),
        out_specs=(P("band", "fft", None), P("band", None)),
        check_vma=False,
    )
```

profile of v0, /device:TPU:1, one launch (start us, length us, event | category | flops | bytes accessed | tf_op | source)
XLA Modules:
  0.0 88.3 jit_solution(14840660237025882449)
XLA Ops:
  1.3 85.2 %shard_map.95 = (f32[288,128]{1,0:T(8,128)}, f32[1,128]{1,0:T(1,128)}) custom-call(s32[1]{0:T(128)S(6)} %copy.10.picked_ref, s32[64]{0:T(128)} %shells_ref.1, f32[162,4,216]{2,1,0:T(4,128)} %bitcast.3, bf16[448,216]{1,0:T(8,128)(2,1)} %constant.10.clone.forward_far, bf16[448,216]{1,0:T(8,128)(2,1)} %constant.11.clone.inverse_far, ...), custom_call_target="tpu_custom_call" | custom-call | tf_op jit(solution)/shard_map/pallas_call | solution.py:596
  86.5 1.8 %shard_map.96 = (f32[162,1,216]{2,1,0:T(1,128)}, f32[1,4]{1,0:T(1,128)}) custom-call(f32[288,128]{1,0:T(8,128)} %get-tuple-element.6.total_ref, f32[1,128]{1,0:T(1,128)} %get-tuple-element.7.row_ref), custom_call_target="tpu_custom_call" | custom-call | tf_op jit(solution)/shard_map/pallas_call | solution.py:635
where the time goes:
time: 88.4 us; the launch traced here: 88.3 us
  Pallas kernels  87 us (98%)
  between operations  1.28 us (1%)
    pallas_call x1, Pallas kernels, body(): pl.pallas_call(whole_kernel, out_shape=(shape(288, 128), shape(1, 128)),...  85.2 us

commit v1 on v0

--- a/solution.py
+++ b/solution.py
@@ -29,7 +29,7 @@
 MESH = pl.DeviceIdType.MESH
 F32 = jnp.float32
 BF16 = jnp.bfloat16
-VMEM_LIMIT = 60 * 1024 * 1024
+VMEM_LIMIT = 53 * 1024 * 1024
 
 
 def halves(table):
@@ -141,18 +141,14 @@
     return both[:NZ] + both[NZ + 8:2 * NZ + 8] + mm(table_ref[:NZ + 8], low)[:NZ]
 
 
+def turned_band(band, pad_ref):
+    pad_ref[:ROWS, :NZ] = band
+    return pack_field(jnp.transpose(pad_ref[...])[:NZ])
+
+
 def order_bands(picked, orbitals_ref, own_ref, order_ref, pad_ref):
-    pad_ref[...] = jnp.zeros_like(pad_ref)
     for b in range(BLK):
-        pad_ref[:ROWS, :NZ] = orbitals_ref[:, b, :]
-        own_ref[b] = pack_field(jnp.transpose(pad_ref[...])[:NZ])
-    chosen = own_ref[0]
-    for b in range(1, BLK):
-        chosen = jnp.where(picked == b, own_ref[b], chosen)
-    order_ref[0] = chosen
-
-
-def order_others(picked, own_ref, order_ref):
+        own_ref[b] = turned_band(orbitals_ref[:, b, :], pad_ref)
     for j in range(1, BLK):
         order_ref[j] = jnp.where(picked >= j, own_ref[j - 1], own_ref[j])
 
@@ -357,7 +353,7 @@
     partial_ref[...] = row * SPACING**3
 
 
-STEPS = [(far, turned) for turned in range(4) for far in (4, 1, -1, 2, -2, 3, -3)] + [(0, turned) for turned in range(1, 4)]
+STEPS = [((1, -2, 3, -1, 2, -3, 4)[k % 7], (0, 2, 1, 3)[k % 4]) for k in range(28)] + [(0, turned) for turned in (2, 1, 3)]
 
 
 class Ring:
@@ -441,10 +437,11 @@
         one.start()
     picked = picked_ref[0]
     fetches[0].wait()
-    order_bands(picked, orbitals_ref, own, order, pad)
+    pad[...] = jnp.zeros_like(pad)
+    order[0] = turned_band(orbitals_ref[:, picked, :], pad)
     pl.semaphore_wait(barrier, FFT + 1)
     chosen_up.start()
-    order_others(picked, own, order)
+    order_bands(picked, orbitals_ref, own, order, pad)
 
     def gain_step(plane, carry):
         gain_of(me, plane, shells_ref, xy_ref, gain)
@@ -452,9 +449,9 @@
 
     for one in fetches[1:]:
         one.wait()
-    lax.fori_loop(0, 6, gain_step, 0)
+    lax.fori_loop(0, 3, gain_step, 0)
     chosen_down.start()
-    lax.fori_loop(6, 10, gain_step, 0)
+    lax.fori_loop(3, 10, gain_step, 0)
     tails[pl.ds(NZ * FIELDS, 24), :] = jnp.zeros((24, 128), F32)
     put_rows(sent, NZ * FIELDS + 256, jnp.zeros((24, 128), F32))
 
@@ -596,7 +593,7 @@
     total, row = pl.pallas_call(
         whole_kernel,
         out_shape=(shape(288, 128), shape(1, 128)),
-        in_specs=[sm(), sm()] + [pl.BlockSpec(memory_space=pl.ANY)] * 6,
+        in_specs=[sm(), sm()] + [pl.BlockSpec(memory_space=pltpu.HBM)] * 6,
         out_specs=(vm(), vm()),
         scratch_shapes=[
             pltpu.VMEM((ROWS, BLK, NZ), F32),

time: 88.4 us -> 91.4 us (1.034)
  local copies, waits for them, and re-layouts: 0 us -> 4.18 us
  Pallas kernels: 87 us -> 85.6 us
    unnamed x0 -> x10, local copies, waits for them, and re-layouts: none -> 4.18 us
where the time goes in v1:
time: 91.4 us; the launch traced here: 91.1 us
  Pallas kernels  85.6 us (94%)
  local copies, waits for them, and re-layouts  4.18 us (5%)
  between operations  1.3 us (1%)
    pallas_call x1, Pallas kernels, body(): pl.pallas_call(whole_kernel, out_shape=(shape(288, 128), shape(1, 128)),...  84.8 us
    unnamed x10, local copies, waits for them, and re-layouts  4.18 us

profile of v1, /device:TPU:1, one launch (start us, length us, event | category | flops | bytes accessed | tf_op | source)
XLA Modules:
  0.0 91.1 jit_solution(3560902517134211115)
XLA Ops:
  1.3 0.0 copy-start.4
  1.3 0.6 copy-done.4
  1.9 0.0 copy-start
  1.9 0.9 %copy-done = bf16[448,216]{1,0:T(8,128)(2,1)S(1)} copy-done((bf16[448,216]{1,0:T(8,128)(2,1)S(1)}, bf16[448,216]{1,0:T(8,128)(2,1)}, u32[]{:S(2)}) %copy-start) | copy-done | bytes 193560
  2.9 0.0 copy-start.1
  2.9 0.9 %copy-done.1 = bf16[448,216]{1,0:T(8,128)(2,1)S(1)} copy-done((bf16[448,216]{1,0:T(8,128)(2,1)S(1)}, bf16[448,216]{1,0:T(8,128)(2,1)}, u32[]{:S(2)}) %copy-start.1) | copy-done | bytes 193560
  3.8 0.0 copy-start.2
  3.8 0.9 copy-done.2
  4.7 0.0 copy-start.3
  4.7 0.8 copy-done.3
  5.5 84.8 %shard_map.95 = (f32[288,128]{1,0:T(8,128)S(1)}, f32[1,128]{1,0:T(1,128)S(1)}) custom-call(s32[1]{0:T(128)S(6)} %copy.10.picked_ref, s32[64]{0:T(128)S(1)} %copy-done.4, f32[162,4,216]{2,1,0:T(4,128)} %bitcast.3, bf16[448,216]{1,0:T(8,128)(2,1)S(1)} %copy-done.1, bf16[448,216]{1,0:T(8,128)(2,1)S(1)} %copy-done, f32[72,128]{1,0:T(8,128)S(1)} %copy-done.3, ...), custom_call_target="tpu_custom_call" | custom-call | tf_op jit(solution)/shard_map/pallas_call | solution.py:593
  90.2 0.9 shard_map.96
Async XLA Ops:
  1.3 0.7 copy-start.4
  1.9 0.9 %copy-start = (bf16[448,216]{1,0:T(8,128)(2,1)S(1)}, bf16[448,216]{1,0:T(8,128)(2,1)}, u32[]{:S(2)}) copy-start(bf16[448,216]{1,0:T(8,128)(2,1)} %constant.11.clone.inverse_far) | copy-start | bytes 580612
  2.9 0.9 %copy-start.1 = (bf16[448,216]{1,0:T(8,128)(2,1)S(1)}, bf16[448,216]{1,0:T(8,128)(2,1)}, u32[]{:S(2)}) copy-start(bf16[448,216]{1,0:T(8,128)(2,1)} %constant.10.clone.forward_far) | copy-start | bytes 580612
  3.8 0.9 copy-start.2
  4.7 0.8 copy-start.3

commit v2 on v1

--- a/solution.py
+++ b/solution.py
@@ -29,7 +29,7 @@
 MESH = pl.DeviceIdType.MESH
 F32 = jnp.float32
 BF16 = jnp.bfloat16
-VMEM_LIMIT = 53 * 1024 * 1024
+VMEM_LIMIT = 60 * 1024 * 1024
 
 
 def halves(table):
@@ -373,11 +373,13 @@
             device_id={"fft": peer}, device_id_type=MESH,
         )
 
-    def start(self, chunk, first, count, k):
+    def start(self, chunk, first, count, k, low=0, high=FFT - 1):
         rows = pl.ds(first, count)
-        for far, turned in STEPS:
+        for far, turned in STEPS[low:high]:
             peer = self.device(far, turned)
             self.copy(self.source.at[chunk, peer, rows], self.target.at[chunk, self.me, rows], peer, k).start()
+        if high < FFT - 1:
+            return
         self.target[chunk, self.me, first:first + count] = self.source[chunk, self.me, first:first + count]
 
     def wait_recv(self, chunk, first, count, k):
@@ -477,8 +479,7 @@
         if chunk == 0:
             home.start(0, 0, 4, 0)
         else:
-            home.start(1, 0, 3, 1)
-            home.start(1, 3, 1, 2)
+            home.start(1, 0, 3, 1, 0, 20)
 
     home.wait_recv(0, 0, 4, 0)
     open_tails(0, returned, tails)
@@ -489,6 +490,8 @@
         total = term if total is None else total + term
     down[...] = total
     sum_down.start()
+    home.start(1, 0, 3, 1, 20)
+    home.start(1, 3, 1, 2)
 
     def up_part(rows, fields):
         total = None

time: 91.4 us -> 88.5 us (0.968)
  local copies, waits for them, and re-layouts: 4.18 us -> 0 us
  Pallas kernels: 85.6 us -> 87.1 us
    unnamed x10 -> x0, local copies, waits for them, and re-layouts: 4.18 us -> none
where the time goes in v2:
time: 88.5 us; the launch traced here: 88.3 us
  Pallas kernels  87.1 us (98%)
  between operations  1.28 us (1%)
    pallas_call x1, Pallas kernels, body(): pl.pallas_call(whole_kernel, out_shape=(shape(288, 128), shape(1, 128)),...  85.3 us

profile of v2, /device:TPU:1, one launch (start us, length us, event | category | flops | bytes accessed | tf_op | source)
XLA Modules:
  0.0 88.3 jit_solution(17989051662838006262)
XLA Ops:
  1.3 85.3 %shard_map.95 = (f32[288,128]{1,0:T(8,128)}, f32[1,128]{1,0:T(1,128)}) custom-call(s32[1]{0:T(128)S(6)} %copy.10.picked_ref, s32[64]{0:T(128)} %shells_ref.1, f32[162,4,216]{2,1,0:T(4,128)} %bitcast.3, bf16[448,216]{1,0:T(8,128)(2,1)} %constant.10.clone.forward_far, bf16[448,216]{1,0:T(8,128)(2,1)} %constant.11.clone.inverse_far, ...), custom_call_target="tpu_custom_call" | custom-call | tf_op jit(solution)/shard_map/pallas_call | solution.py:596
  86.6 1.8 %shard_map.96 = (f32[162,1,216]{2,1,0:T(1,128)}, f32[1,4]{1,0:T(1,128)}) custom-call(f32[288,128]{1,0:T(8,128)} %get-tuple-element.6.total_ref, f32[1,128]{1,0:T(1,128)} %get-tuple-element.7.row_ref), custom_call_target="tpu_custom_call" | custom-call | tf_op jit(solution)/shard_map/pallas_call | solution.py:635

commit v3 on v2

--- a/solution.py
+++ b/solution.py
@@ -449,11 +449,9 @@
         gain_of(me, plane, shells_ref, xy_ref, gain)
         return carry
 
+    chosen_down.start()
     for one in fetches[1:]:
         one.wait()
-    lax.fori_loop(0, 3, gain_step, 0)
-    chosen_down.start()
-    lax.fori_loop(3, 10, gain_step, 0)
     tails[pl.ds(NZ * FIELDS, 24), :] = jnp.zeros((24, 128), F32)
     put_rows(sent, NZ * FIELDS + 256, jnp.zeros((24, 128), F32))
 
@@ -469,7 +467,7 @@
         spectrum_of(f, order, upper, lower, forward_ref, sent, tails)
     close_tails(1, sent, tails)
     there.start(1, 0, 4, 1)
-    lax.fori_loop(10, 2 * PLANES, gain_step, 0)
+    lax.fori_loop(0, 2 * PLANES, gain_step, 0)
 
     for chunk in range(2):
         there.wait_recv(chunk, 0, 4, chunk)

time: 88.5 us -> 88.6 us (level)
  no operation moved by 1% of the time
where the time goes in v3:
time: 88.6 us; the launch traced here: 88.5 us
  Pallas kernels  87.2 us (98%)
  between operations  1.28 us (1%)
    pallas_call x1, Pallas kernels, body(): pl.pallas_call(whole_kernel, out_shape=(shape(288, 128), shape(1, 128)),...  85.5 us

profile of v3, /device:TPU:1, one launch (start us, length us, event | category | flops | bytes accessed | tf_op | source)
XLA Modules:
  0.0 88.5 jit_solution(8709115870908517330)
XLA Ops:
  1.3 85.5 %shard_map.95 = (f32[288,128]{1,0:T(8,128)}, f32[1,128]{1,0:T(1,128)}) custom-call(s32[1]{0:T(128)S(6)} %copy.10.picked_ref, s32[64]{0:T(128)} %shells_ref.1, f32[162,4,216]{2,1,0:T(4,128)} %bitcast.3, bf16[448,216]{1,0:T(8,128)(2,1)} %constant.10.clone.forward_far, bf16[448,216]{1,0:T(8,128)(2,1)} %constant.11.clone.inverse_far, ...), custom_call_target="tpu_custom_call" | custom-call | tf_op jit(solution)/shard_map/pallas_call | solution.py:594
  86.7 1.8 %shard_map.96 = (f32[162,1,216]{2,1,0:T(1,128)}, f32[1,4]{1,0:T(1,128)}) custom-call(f32[288,128]{1,0:T(8,128)} %get-tuple-element.6.total_ref, f32[1,128]{1,0:T(1,128)} %get-tuple-element.7.row_ref), custom_call_target="tpu_custom_call" | custom-call | tf_op jit(solution)/shard_map/pallas_call | solution.py:633

commit v4 on v3

--- a/solution.py
+++ b/solution.py
@@ -353,42 +353,43 @@
     partial_ref[...] = row * SPACING**3
 
 
-STEPS = [((1, -2, 3, -1, 2, -3, 4)[k % 7], (0, 2, 1, 3)[k % 4]) for k in range(28)] + [(0, turned) for turned in (2, 1, 3)]
+AROUND = [((1, -2, 3, -1, 2, -3, 4)[k % 7], (0, 2, 1, 3)[k % 4]) for k in range(28)] + [(0, turned) for turned in (2, 1, 3)]
+STEPS = (AROUND, AROUND + [(0, 0)])
 
 
 class Ring:
-    def __init__(self, me, source, target, send_sem, recv_sem):
+    def __init__(self, me, group, source, target, send_sem, recv_sem):
         self.source, self.target = source, target
         self.send_sem, self.recv_sem = send_sem, recv_sem
         self.me = me
+        self.groups = [group, group + 1 - 2 * lax.rem(group, 2)]
         self.places = [lax.rem(me // 4 + k, 8) for k in range(8)]
         self.parts = [lax.rem(lax.rem(me, 4) + k, 4) for k in range(4)]
 
-    def device(self, far, turned):
-        return 4 * self.places[far % 8] + self.parts[turned % 4]
+    def device(self, chunk, far, turned):
+        return {"band": self.groups[chunk], "fft": 4 * self.places[far % 8] + self.parts[turned % 4]}
 
     def copy(self, source, target, peer, k):
         return pltpu.make_async_remote_copy(
             src_ref=source, dst_ref=target, send_sem=self.send_sem.at[k], recv_sem=self.recv_sem.at[k],
-            device_id={"fft": peer}, device_id_type=MESH,
+            device_id=peer, device_id_type=MESH,
         )
 
-    def start(self, chunk, first, count, k, low=0, high=FFT - 1):
+    def start(self, chunk, first, count, k, low=0, high=FFT):
         rows = pl.ds(first, count)
-        for far, turned in STEPS[low:high]:
-            peer = self.device(far, turned)
-            self.copy(self.source.at[chunk, peer, rows], self.target.at[chunk, self.me, rows], peer, k).start()
-        if high < FFT - 1:
-            return
-        self.target[chunk, self.me, first:first + count] = self.source[chunk, self.me, first:first + count]
+        for far, turned in STEPS[chunk][low:high]:
+            peer = self.device(chunk, far, turned)
+            self.copy(self.source.at[chunk, peer["fft"], rows], self.target.at[chunk, self.me, rows], peer, k).start()
+        if chunk == 0:
+            self.target[chunk, self.me, first:first + count] = self.source[chunk, self.me, first:first + count]
 
     def wait_recv(self, chunk, first, count, k):
-        whole = self.target.at[chunk, pl.ds(0, FFT - 1), pl.ds(first, count)]
-        self.copy(whole, whole, self.device(1, 0), k).wait_recv()
+        whole = self.target.at[chunk, pl.ds(0, len(STEPS[chunk])), pl.ds(first, count)]
+        self.copy(whole, whole, self.device(chunk, 1, 0), k).wait_recv()
 
     def wait_send(self, chunk, first, count, k):
-        whole = self.source.at[chunk, pl.ds(0, FFT - 1), pl.ds(first, count)]
-        self.copy(whole, whole, self.device(1, 0), k).wait_send()
+        whole = self.source.at[chunk, pl.ds(0, len(STEPS[chunk])), pl.ds(first, count)]
+        self.copy(whole, whole, self.device(chunk, 1, 0), k).wait_send()
 
 
 def whole_kernel(
@@ -407,11 +408,11 @@
     barrier = pltpu.get_barrier_semaphore()
     for peer in (above_me, below_me):
         pl.semaphore_signal(barrier, inc=1, device_id={"band": peer}, device_id_type=MESH)
-    there = Ring(me, sent, got, there_send, there_recv)
-    home = Ring(me, back, returned, home_send, home_recv)
-    for far, turned in STEPS:
-        peer = there.device(far, turned)
-        pl.semaphore_signal(barrier, inc=1, device_id={"fft": peer}, device_id_type=MESH)
+    there = Ring(me, group, sent, got, there_send, there_recv)
+    home = Ring(me, group, back, returned, home_send, home_recv)
+    for chunk in range(2):
+        for far, turned in AROUND:
+            pl.semaphore_signal(barrier, inc=1, device_id=there.device(chunk, far, turned), device_id_type=MESH)
 
     def to_band(source, target, peer, k):
         return pltpu.make_async_remote_copy(
@@ -441,7 +442,7 @@
     fetches[0].wait()
     pad[...] = jnp.zeros_like(pad)
     order[0] = turned_band(orbitals_ref[:, picked, :], pad)
-    pl.semaphore_wait(barrier, FFT + 1)
+    pl.semaphore_wait(barrier, 2 * FFT)
     chosen_up.start()
     order_bands(picked, orbitals_ref, own, order, pad)
 

time: 88.6 us -> 88.3 us (level)
  the two profiles are of different devices: /device:TPU:1 before, /device:TPU:14 now
where the time goes in v4:
time: 88.3 us; the launch traced here: 88.2 us
  Pallas kernels  86.9 us (98%)
  between operations  1.28 us (1%)
    pallas_call x1, Pallas kernels, body(): pl.pallas_call(whole_kernel, out_shape=(shape(288, 128), shape(1, 128)),...  85.1 us
    pallas_call x1, Pallas kernels, body(): pl.pallas_call(last_kernel, out_shape=(shape(ROWS, 1, NZ), shape(1, BLK))...  1.77 us

profile of v4, /device:TPU:14, one launch (start us, length us, event | category | flops | bytes accessed | tf_op | source)
XLA Modules:
  0.0 88.2 jit_solution(18379932591004184000)
XLA Ops:
  1.3 85.1 %shard_map.95 = (f32[288,128]{1,0:T(8,128)}, f32[1,128]{1,0:T(1,128)}) custom-call(s32[1]{0:T(128)S(6)} %copy.10.picked_ref, s32[64]{0:T(128)} %shells_ref.1, f32[162,4,216]{2,1,0:T(4,128)} %bitcast.3, bf16[448,216]{1,0:T(8,128)(2,1)} %constant.10.clone.forward_far, bf16[448,216]{1,0:T(8,128)(2,1)} %constant.11.clone.inverse_far, ...), custom_call_target="tpu_custom_call" | custom-call | tf_op jit(solution)/shard_map/pallas_call | solution.py:595
  86.4 1.8 %shard_map.96 = (f32[162,1,216]{2,1,0:T(1,128)}, f32[1,4]{1,0:T(1,128)}) custom-call(f32[288,128]{1,0:T(8,128)} %get-tuple-element.6.total_ref, f32[1,128]{1,0:T(1,128)} %get-tuple-element.7.row_ref), custom_call_target="tpu_custom_call" | custom-call | tf_op jit(solution)/shard_map/pallas_call | solution.py:634

commit v5 on v4

--- a/solution.py
+++ b/solution.py
@@ -380,7 +380,7 @@
         for far, turned in STEPS[chunk][low:high]:
             peer = self.device(chunk, far, turned)
             self.copy(self.source.at[chunk, peer["fft"], rows], self.target.at[chunk, self.me, rows], peer, k).start()
-        if chunk == 0:
+        if chunk == 0 and high == FFT:
             self.target[chunk, self.me, first:first + count] = self.source[chunk, self.me, first:first + count]
 
     def wait_recv(self, chunk, first, count, k):
@@ -472,11 +472,13 @@
 
     for chunk in range(2):
         there.wait_recv(chunk, 0, 4, chunk)
+        if chunk == 1:
+            home.start(0, 0, 4, 0, 8)
         open_rows(got, chunk, box)
         screen_planes(me, chunk, x_ref, y_ref, box, work, gain)
         close_rows(box, chunk, back)
         if chunk == 0:
-            home.start(0, 0, 4, 0)
+            home.start(0, 0, 4, 0, 0, 8)
         else:
             home.start(1, 0, 3, 1, 0, 20)
 

time: 88.3 us -> 89.1 us (level)
  the two profiles are of different devices: /device:TPU:14 before, /device:TPU:1 now
where the time goes in v5:
time: 89.1 us; the launch traced here: 88.9 us
  Pallas kernels  87.7 us (98%)
  between operations  1.28 us (1%)
    pallas_call x1, Pallas kernels, body(): pl.pallas_call(whole_kernel, out_shape=(shape(288, 128), shape(1, 128)),...  85.9 us

profile of v5, /device:TPU:1, one launch (start us, length us, event | category | flops | bytes accessed | tf_op | source)
XLA Modules:
  0.0 88.9 jit_solution(10475003977832366131)
XLA Ops:
  1.3 85.9 %shard_map.95 = (f32[288,128]{1,0:T(8,128)}, f32[1,128]{1,0:T(1,128)}) custom-call(s32[1]{0:T(128)S(6)} %copy.10.picked_ref, s32[64]{0:T(128)} %shells_ref.1, f32[162,4,216]{2,1,0:T(4,128)} %bitcast.3, bf16[448,216]{1,0:T(8,128)(2,1)} %constant.10.clone.forward_far, bf16[448,216]{1,0:T(8,128)(2,1)} %constant.11.clone.inverse_far, ...), custom_call_target="tpu_custom_call" | custom-call | tf_op jit(solution)/shard_map/pallas_call | solution.py:597
  87.2 1.8 %shard_map.96 = (f32[162,1,216]{2,1,0:T(1,128)}, f32[1,4]{1,0:T(1,128)}) custom-call(f32[288,128]{1,0:T(8,128)} %get-tuple-element.6.total_ref, f32[1,128]{1,0:T(1,128)} %get-tuple-element.7.row_ref), custom_call_target="tpu_custom_call" | custom-call | tf_op jit(solution)/shard_map/pallas_call | solution.py:636

commit v6 on v4

--- a/solution.py
+++ b/solution.py
@@ -394,7 +394,7 @@
 
 def whole_kernel(
     picked_ref, shells_ref, orbitals_far, forward_far, inverse_far, xy_far, x_far, y_far,
-    total_ref, result_ref,
+    result_ref,
     orbitals_ref, forward_ref, inverse_ref, xy_ref, x_ref, y_ref, fetch_sem,
     own, order, upper, lower, up, down, above, below, mine, sent, got, back, returned, tails, box, work, gain, pad,
     partial, ring_slots, near, near_slots,
@@ -478,7 +478,7 @@
         if chunk == 0:
             home.start(0, 0, 4, 0)
         else:
-            home.start(1, 0, 3, 1, 0, 20)
+            home.start(1, 0, 4, 1, 0, 20)
 
     home.wait_recv(0, 0, 4, 0)
     open_tails(0, returned, tails)
@@ -489,8 +489,7 @@
         total = term if total is None else total + term
     down[...] = total
     sum_down.start()
-    home.start(1, 0, 3, 1, 20)
-    home.start(1, 3, 1, 2)
+    home.start(1, 0, 4, 1, 20)
 
     def up_part(rows, fields):
         total = None
@@ -501,10 +500,9 @@
             total = term if total is None else total + term
         up[rows, :] = total
 
-    home.wait_recv(1, 0, 3, 1)
+    home.wait_recv(1, 0, 4, 1)
     up_part(main, [(f, z_transform(inverse_ref, main_of(f, returned))) for f in range(3, FIELDS)])
     sum_up_main.start()
-    home.wait_recv(1, 3, 1, 2)
     open_tails(1, returned, tails)
     up_part(tail, [(f, pack_thirds(z_transform(inverse_ref, tail_of(f, tails)))) for f in range(3, FIELDS)])
     sum_up_tail.start()
@@ -513,7 +511,7 @@
     sum_up_main.wait_recv()
     sum_up_tail.wait_recv()
     total = mine[...] + below[...]
-    total_ref[...] = total
+    result_ref[:288, :] = total
     intersect(total, own, partial)
 
     place, part = me // 4, lax.rem(me, 4)
@@ -544,22 +542,21 @@
     for k, one in enumerate(beside):
         one.wait()
         row = row + near_slots[k + 1]
-    result_ref[...] = row
+    result_ref[288:, :] = jnp.broadcast_to(row, (8, 128))
 
     there.wait_send(0, 0, 4, 0)
     there.wait_send(1, 0, 4, 1)
     home.wait_send(0, 0, 4, 0)
-    home.wait_send(1, 0, 3, 1)
-    home.wait_send(1, 3, 1, 2)
+    home.wait_send(1, 0, 4, 1)
     for one in (chosen_up, chosen_down, sum_down, sum_up_main, sum_up_tail):
         one.wait_send()
 
 
-def last_kernel(total_ref, row_ref, potential_ref, result_ref, pad_ref):
+def last_kernel(given_ref, potential_ref, result_ref, pad_ref):
     pad_ref[...] = jnp.zeros_like(pad_ref)
-    pad_ref[:NZ, :] = unpack_field(total_ref[...])
+    pad_ref[:NZ, :] = unpack_field(given_ref[:288, :])
     potential_ref[:, 0, :] = jnp.transpose(pad_ref[...])[:ROWS, :NZ]
-    row = row_ref[...]
+    row = given_ref[288:289, :]
     lane = lanes((1, BLK))
     result = jnp.zeros((1, BLK), F32)
     for b in range(BLK):
@@ -592,11 +589,11 @@
     bands = pltpu.VMEM((BLK, 288, 128), F32)
     line = pltpu.VMEM((1, 128), F32)
     dma = pltpu.SemaphoreType.DMA
-    total, row = pl.pallas_call(
+    given = pl.pallas_call(
         whole_kernel,
-        out_shape=(shape(288, 128), shape(1, 128)),
+        out_shape=shape(296, 128),
         in_specs=[sm(), sm()] + [pl.BlockSpec(memory_space=pltpu.HBM)] * 6,
-        out_specs=(vm(), vm()),
+        out_specs=vm(),
         scratch_shapes=[
             pltpu.VMEM((ROWS, BLK, NZ), F32),
             pltpu.VMEM(forward.shape, BF16),
@@ -622,7 +619,7 @@
             pltpu.VMEM((4, 1, 128), F32),
         ]
         + [dma((2,))] * 2
-        + [dma((3,))] * 2
+        + [dma((2,))] * 2
         + [dma((5,))] * 2
         + [dma((8,))] * 2
         + [dma((4,))] * 2,
@@ -634,11 +631,11 @@
     potentials, result = pl.pallas_call(
         last_kernel,
         out_shape=(shape(ROWS, 1, NZ), shape(1, BLK)),
-        in_specs=[vm()] * 2,
+        in_specs=[vm()],
         out_specs=(vm(), vm()),
         scratch_shapes=[pltpu.VMEM((256, 256), F32)],
         compiler_params=params(),
-    )(total, row)
+    )(given)
     return jnp.transpose(potentials, (1, 0, 2)), jnp.transpose(result)
 
 

time: 88.3 us -> 88.1 us (level)
  the two profiles are of different devices: /device:TPU:14 before, /device:TPU:12 now
where the time goes in v6:
time: 88.1 us; the launch traced here: 88 us
  Pallas kernels  86.7 us (98%)
  between operations  1.28 us (1%)
    pallas_call x1, Pallas kernels, body(): pl.pallas_call(whole_kernel, out_shape=shape(296, 128), in_specs=[sm(), s...  84.9 us
    pallas_call x1, Pallas kernels, body(): pl.pallas_call(last_kernel, out_shape=(shape(ROWS, 1, NZ), shape(1, BLK))...  1.77 us

profile of v6, /device:TPU:12, one launch (start us, length us, event | category | flops | bytes accessed | tf_op | source)
XLA Modules:
  0.0 88.0 jit_solution(8479902949961074902)
XLA Ops:
  1.3 84.9 %shard_map.95.given_ref = f32[296,128]{1,0:T(8,128)} custom-call(s32[1]{0:T(128)S(6)} %copy.10.picked_ref, s32[64]{0:T(128)} %shells_ref.1, f32[162,4,216]{2,1,0:T(4,128)} %bitcast.3, bf16[448,216]{1,0:T(8,128)(2,1)} %constant.10.clone.forward_far, bf16[448,216]{1,0:T(8,128)(2,1)} %constant.11.clone.inverse_far, f32[72,128]{1,0:T(8,128)} %constant.12.clone.xy_far, ...), custom_call_target="tpu_custom_call" | custom-call | tf_op jit(solution)/shard_map/pallas_call | solution.py:592
  86.2 1.8 %shard_map.96 = (f32[162,1,216]{2,1,0:T(1,128)}, f32[1,4]{1,0:T(1,128)}) custom-call(f32[296,128]{1,0:T(8,128)} %shard_map.95.given_ref), custom_call_target="tpu_custom_call" | custom-call | tf_op jit(solution)/shard_map/pallas_call | solution.py:631

commit v7 on v6

--- a/solution.py
+++ b/solution.py
@@ -459,11 +459,10 @@
     chosen_up.wait_recv()
     for f in range(3):
         spectrum_of(f, order, upper, lower, forward_ref, sent, tails)
-    there.start(0, 0, 2, 0)
     chosen_down.wait_recv()
     spectrum_of(3, order, upper, lower, forward_ref, sent, tails)
     close_tails(0, sent, tails)
-    there.start(0, 2, 2, 0)
+    there.start(0, 0, 4, 0)
     for f in range(4, FIELDS):
         spectrum_of(f, order, upper, lower, forward_ref, sent, tails)
     close_tails(1, sent, tails)

time: 88.1 us -> 89.8 us (1.019)
  the two profiles are of different devices: /device:TPU:12 before, /device:TPU:1 now
where the time goes in v7:
time: 89.8 us; the launch traced here: 89.7 us
  Pallas kernels  88.4 us (98%)
  between operations  1.28 us (1%)
    pallas_call x1, Pallas kernels, body(): pl.pallas_call(whole_kernel, out_shape=shape(296, 128), in_specs=[sm(), s...  86.6 us

profile of v7, /device:TPU:1, one launch (start us, length us, event | category | flops | bytes accessed | tf_op | source)
XLA Modules:
  0.0 89.7 jit_solution(14990045840790673630)
XLA Ops:
  1.3 86.6 %shard_map.95.given_ref = f32[296,128]{1,0:T(8,128)} custom-call(s32[1]{0:T(128)S(6)} %copy.10.picked_ref, s32[64]{0:T(128)} %shells_ref.1, f32[162,4,216]{2,1,0:T(4,128)} %bitcast.3, bf16[448,216]{1,0:T(8,128)(2,1)} %constant.10.clone.forward_far, bf16[448,216]{1,0:T(8,128)(2,1)} %constant.11.clone.inverse_far, f32[72,128]{1,0:T(8,128)} %constant.12.clone.xy_far, ...), custom_call_target="tpu_custom_call" | custom-call | tf_op jit(solution)/shard_map/pallas_call | solution.py:591
  87.9 1.8 %shard_map.96 = (f32[162,1,216]{2,1,0:T(1,128)}, f32[1,4]{1,0:T(1,128)}) custom-call(f32[296,128]{1,0:T(8,128)} %shard_map.95.given_ref), custom_call_target="tpu_custom_call" | custom-call | tf_op jit(solution)/shard_map/pallas_call | solution.py:630

commit v8 on v6

--- a/solution.py
+++ b/solution.py
@@ -450,9 +450,10 @@
         gain_of(me, plane, shells_ref, xy_ref, gain)
         return carry
 
-    chosen_down.start()
     for one in fetches[1:]:
         one.wait()
+    lax.fori_loop(0, 3, gain_step, 0)
+    chosen_down.start()
     tails[pl.ds(NZ * FIELDS, 24), :] = jnp.zeros((24, 128), F32)
     put_rows(sent, NZ * FIELDS + 256, jnp.zeros((24, 128), F32))
 
@@ -468,7 +469,7 @@
         spectrum_of(f, order, upper, lower, forward_ref, sent, tails)
     close_tails(1, sent, tails)
     there.start(1, 0, 4, 1)
-    lax.fori_loop(0, 2 * PLANES, gain_step, 0)
+    lax.fori_loop(3, 2 * PLANES, gain_step, 0)
 
     for chunk in range(2):
         there.wait_recv(chunk, 0, 4, chunk)

time: 88.1 us -> 88.3 us (level)
  no operation moved by 1% of the time
where the time goes in v8:
time: 88.3 us; the launch traced here: 88.2 us
  Pallas kernels  86.9 us (98%)
  between operations  1.28 us (1%)
    pallas_call x1, Pallas kernels, body(): pl.pallas_call(whole_kernel, out_shape=shape(296, 128), in_specs=[sm(), s...  85.1 us
    pallas_call x1, Pallas kernels, body(): pl.pallas_call(last_kernel, out_shape=(shape(ROWS, 1, NZ), shape(1, BLK))...  1.77 us

profile of v8, /device:TPU:12, one launch (start us, length us, event | category | flops | bytes accessed | tf_op | source)
XLA Modules:
  0.0 88.2 jit_solution(18364605871073237171)
XLA Ops:
  1.3 85.1 %shard_map.95.given_ref = f32[296,128]{1,0:T(8,128)} custom-call(s32[1]{0:T(128)S(6)} %copy.10.picked_ref, s32[64]{0:T(128)} %shells_ref.1, f32[162,4,216]{2,1,0:T(4,128)} %bitcast.3, bf16[448,216]{1,0:T(8,128)(2,1)} %constant.10.clone.forward_far, bf16[448,216]{1,0:T(8,128)(2,1)} %constant.11.clone.inverse_far, f32[72,128]{1,0:T(8,128)} %constant.12.clone.xy_far, ...), custom_call_target="tpu_custom_call" | custom-call | tf_op jit(solution)/shard_map/pallas_call | solution.py:593
  86.4 1.8 %shard_map.96 = (f32[162,1,216]{2,1,0:T(1,128)}, f32[1,4]{1,0:T(1,128)}) custom-call(f32[296,128]{1,0:T(8,128)} %shard_map.95.given_ref), custom_call_target="tpu_custom_call" | custom-call | tf_op jit(solution)/shard_map/pallas_call | solution.py:632
